TPU v7x, 512 devices: a whole 4x4x16 slice. The times are simulated.
512 devices in a mesh: slab: 16 (over x_lo, y, core), coef: 32 (over x_hi, z).
Axes of the slice: x: 4 (x_hi: 2, x_lo: 2; x = x_hi * 2 + x_lo), y: 4, z: 16, core: 2. Of those that a mesh axis runs over, the one named last changes fastest.
Arguments:
- cotangent: float32 [8192, 4096], P('slab', 'coef'), may hold values from -6 to 6
- transport_state: bfloat16 [8192, 4096], P('slab', 'coef'), may hold values from -6 to 6
- source_state: bfloat16 [8192, 4096], P('slab', 'coef'), may hold values from -6 to 6
- courant: float32 [8192], P('slab'), may hold values from 0.2 to 1.2
- upwind_codes: int32 [8192], P('slab'), may hold values from 0 to 1
- strain_rate: float32 [9, 8192], P(None, ('slab', 'coef')), may hold values from -4 to 4
Outputs:
- adj_source: float32 [8192, 4096], P('slab', 'coef')
- adj_strain: float32 [9, 8192], P(None, ('slab', 'coef'))
- adj_courant: float32 [8192], P(('slab', 'coef'))
All inputs are finite; a program needn't handle non-finite values.
Results may differ from a plain program's by a relative error of at most 0.0003.
Values may be sent and summed in bfloat16 or wider, within the bound.
A program may use at most 64 MiB of HBM per device.

v0:
```python
import math
import jax
import jax.numpy as jnp
from jax import lax
from jax.sharding import PartitionSpec as P

CYZ = 128
NH = 16
QP = 24
K = 4096
section_weights = (0.25, 1.0 / 3.0, 0.5, 1.0)
quad_half = 4.5
fene_limit = 64.0
time_step = 0.005
highest = lax.Precision.HIGHEST
pair_rows = (0, 1, 2, 4, 5, 8)
pair_slots = (0, 1, 2, 1, 3, 4, 2, 4, 5)


def extended(block, sides, width):
    for axis, dim in sides:
        count = lax.axis_size(axis)
        forward = [(i, i + 1) for i in range(count - 1)]
        forward.append((count - 1, 0))
        backward = [(target, source) for source, target in forward]
        low = lax.ppermute(
            lax.slice_in_dim(block, block.shape[dim] - width, None, axis=dim), axis, forward
        )
        high = lax.ppermute(lax.slice_in_dim(block, 0, width, axis=dim), axis, backward)
        block = jnp.concatenate([low, block, high], axis=dim)
    return block


def shifted(shard, axis, by):
    count = lax.axis_size(axis)
    return lax.ppermute(shard, axis, [(i, (i + by) % count) for i in range(count)])


def hermite_table(mode_count, points):
    node_list = quad_half * (2.0 * jnp.arange(points, dtype=jnp.float32) + 1.0 - points) / points
    leading = jnp.exp(-0.5 * node_list * node_list) * math.pi ** (-0.25)
    table_rows = [leading, math.sqrt(2.0) * node_list * leading]
    for degree in range(1, mode_count - 1):
        table_rows.append(
            math.sqrt(2.0 / (degree + 1.0)) * node_list * table_rows[degree]
            - math.sqrt(degree / (degree + 1.0)) * table_rows[degree - 1]
        )
    return (jnp.stack(table_rows[:mode_count]), node_list)


def quadrature_tables(mode_count, points):
    hermite, node_list = hermite_table(mode_count, points)
    cube_shape = (points, points, points)
    coords = (
        jnp.broadcast_to(node_list[:, None, None], cube_shape).reshape(-1),
        jnp.broadcast_to(node_list[None, :, None], cube_shape).reshape(-1),
        jnp.broadcast_to(node_list[None, None, :], cube_shape).reshape(-1),
    )
    spring = (
        1.0 - (coords[0] * coords[0] + coords[1] * coords[1] + coords[2] * coords[2]) / fene_limit
    )
    pair_table = jnp.stack(
        [
            coords[left_dim] * coords[right_dim] / spring
            for left_dim in range(3)
            for right_dim in range(3)
        ]
    )
    return (hermite, pair_table)


def joined_values(coeffs, hermite, kron_table):
    cell_count = coeffs.shape[0]
    mode_count, points = hermite.shape
    inner_part = jnp.dot(
        coeffs.reshape(cell_count * mode_count, mode_count * mode_count),
        kron_table,
        preferred_element_type=jnp.float32,
        precision=highest,
    )
    outer_part = jnp.einsum(
        "cim,ia->cam",
        inner_part.reshape(cell_count, mode_count, points * points),
        hermite,
        precision=highest,
    )
    return outer_part.reshape(cell_count, points**3)


def joined_coefficients(values, hermite, kron_table):
    cell_count = values.shape[0]
    mode_count, points = hermite.shape
    inner_part = jnp.einsum(
        "cam,ia->cim",
        values.reshape(cell_count, points, points * points),
        hermite,
        precision=highest,
    )
    outer_part = jnp.dot(
        inner_part.reshape(cell_count * mode_count, points * points),
        kron_table.T,
        preferred_element_type=jnp.float32,
        precision=highest,
    )
    return outer_part.reshape(cell_count, mode_count**3)


def body(cotangent, transport_state, source_state, courant, upwind_codes, strain_rate):
    row_count, coef_width = cotangent.shape
    plane_count = row_count // CYZ
    grid_shape = (plane_count, CYZ, coef_width)
    speed_grid = courant.reshape(plane_count, CYZ, 1)
    upper_mask = (upwind_codes == 1).astype(jnp.float32).reshape(plane_count, CYZ, 1)
    lower_mask = 1.0 - upper_mask
    initial = transport_state.astype(jnp.float32).reshape(grid_shape)
    differences = []
    section_now = initial
    for section_no in range(4):
        padded = extended(section_now, (("slab", 0),), 1)
        change = lower_mask * (section_now - padded[:-2]) + upper_mask * (padded[2:] - section_now)
        differences.append(change)
        if section_no < 3:
            section_now = initial - section_weights[section_no] * speed_grid * change
    adjoint = cotangent.reshape(grid_shape)
    accumulated = jnp.zeros(grid_shape, jnp.float32)
    speed_part = jnp.zeros((plane_count, CYZ), jnp.float32)
    for section_no in (3, 2, 1, 0):
        speed_part = speed_part - section_weights[section_no] * jnp.sum(
            adjoint * differences[section_no], axis=2
        )
        accumulated = accumulated + adjoint
        weighted = speed_grid * adjoint
        low_part = lower_mask * weighted
        high_part = upper_mask * weighted
        from_above = shifted(low_part[:1], "slab", -1)
        from_below = shifted(high_part[-1:], "slab", 1)
        next_low = jnp.concatenate([low_part[1:], from_above], axis=0)
        prior_high = jnp.concatenate([from_below, high_part[:-1]], axis=0)
        adjoint = -section_weights[section_no] * (low_part - next_low - high_part + prior_high)
    mu_field = (accumulated + adjoint).reshape(row_count, coef_width)
    speed_column = speed_part.reshape(row_count, 1)
    mu_cells, speed_columns = (
        lax.all_to_all(mu_field, "coef", split_axis=0, concat_axis=1, tiled=True),
        lax.all_to_all(speed_column, "coef", split_axis=0, concat_axis=1, tiled=True),
    )
    source_cells = lax.all_to_all(source_state, "coef", split_axis=0, concat_axis=1, tiled=True)
    source_wide = source_cells.astype(jnp.float32)
    adj_courant = jnp.sum(speed_columns, axis=1) / math.sqrt(K)
    hermite, pair_table = quadrature_tables(NH, QP)
    kron_table = (hermite[:, None, :, None] * hermite[None, :, None, :]).reshape(NH * NH, QP * QP)
    weight_cube = (2.0 * quad_half / QP) ** 3
    adj_values = weight_cube * joined_values(mu_cells, hermite, kron_table)
    multiplier = 1.0 + time_step * jnp.einsum(
        "sc,sq->cq", strain_rate, pair_table, precision=highest
    )
    adj_cells = joined_coefficients(multiplier * adj_values, hermite, kron_table)
    unique_table = jnp.stack([pair_table[slot_no] for slot_no in pair_rows])
    source_values = joined_values(source_wide, hermite, kron_table)
    strain_unique = time_step * jnp.einsum(
        "pq,cq->pc", unique_table, adj_values * source_values, precision=highest
    )
    adj_source = lax.all_to_all(adj_cells, "coef", split_axis=1, concat_axis=0, tiled=True)
    adj_strain = jnp.stack([strain_unique[slot_no] for slot_no in pair_slots])
    return (adj_source, adj_strain, adj_courant)


def solution(mesh):
    placed = (
        P("slab", "coef"),
        P("slab", "coef"),
        P("slab", "coef"),
        P("slab"),
        P("slab"),
        P(None, ("slab", "coef")),
    )
    return jax.shard_map(
        body,
        mesh=mesh,
        in_specs=placed,
        out_specs=(P("slab", "coef"), P(None, ("slab", "coef")), P(("slab", "coef"))),
        check_vma=False,
    )
```

profile of v0, /device:TPU:24, one launch (start us, length us, event | category | flops | bytes accessed | tf_op | source)
XLA Modules:
  0.0 190.6 jit_solution(3589017161790618663)
XLA Ops:
  1.7 2.1 %collective-permute-start.9 = (f32[1,128,128]{2,1,0:T(8,128)S(1)}, f32[1,128,128]{2,1,0:T(8,128)S(1)}, u32[]{:S(2)}, u32[]{:S(2)}) collective-permute-start(f32[1,128,128]{2,1,0:T(8,128)S(1)} %get-tuple-element.28), channel_id=1, source_target_pairs={{32,0},{64,32},{96,64},{128,96},{160,128},{192,160},{224,192},{256... | collective-permute-start | bytes 196616 | tf_op jit(solution)/shard_map/ppermute | solution.py:29
  3.8 2.2 %collective-permute-start.8 = (f32[1,128,128]{2,1,0:T(8,128)S(1)}, f32[1,128,128]{2,1,0:T(8,128)S(1)}, u32[]{:S(2)}, u32[]{:S(2)}) collective-permute-start(f32[1,128,128]{2,1,0:T(8,128)S(1)} %get-tuple-element.27), channel_id=1, source_target_pairs={{0,32},{32,64},{64,96},{96,128},{128,160},{160,192},{192,224},{224... | collective-permute-start | bytes 196616 | tf_op jit(solution)/shard_map/ppermute | solution.py:26
  11.1 3.3 %collective-permute-start.11 = (f32[1,128,128]{2,1,0:T(8,128)S(1)}, f32[1,128,128]{2,1,0:T(8,128)S(1)}, u32[]{:S(2)}, u32[]{:S(2)}) collective-permute-start(f32[1,128,128]{2,1,0:T(8,128)S(1)} %get-tuple-element.26), channel_id=1, source_target_pairs={{32,0},{64,32},{96,64},{128,96},{160,128},{192,160},{224,192},{256... | collective-permute-start | bytes 196616 | tf_op jit(solution)/shard_map/ppermute | solution.py:29
  14.4 3.7 %collective-permute-start.10 = (f32[1,128,128]{2,1,0:T(8,128)S(1)}, f32[1,128,128]{2,1,0:T(8,128)S(1)}, u32[]{:S(2)}, u32[]{:S(2)}) collective-permute-start(f32[1,128,128]{2,1,0:T(8,128)S(1)} %get-tuple-element.25), channel_id=1, source_target_pairs={{0,32},{32,64},{64,96},{96,128},{128,160},{160,192},{192,224},{224... | collective-permute-start | bytes 196616 | tf_op jit(solution)/shard_map/ppermute | solution.py:26
  18.7 1.4 collective-permute-done.10
  20.3 1.9 %collective-permute-start.13 = (f32[1,128,128]{2,1,0:T(8,128)S(1)}, f32[1,128,128]{2,1,0:T(8,128)S(1)}, u32[]{:S(2)}, u32[]{:S(2)}) collective-permute-start(f32[1,128,128]{2,1,0:T(8,128)S(1)} %get-tuple-element.24), channel_id=1, source_target_pairs={{32,0},{64,32},{96,64},{128,96},{160,128},{192,160},{224,192},{256... | collective-permute-start | bytes 196616 | tf_op jit(solution)/shard_map/ppermute | solution.py:29
  22.2 5.2 %collective-permute-start.12 = (f32[1,128,128]{2,1,0:T(8,128)S(1)}, f32[1,128,128]{2,1,0:T(8,128)S(1)}, u32[]{:S(2)}, u32[]{:S(2)}) collective-permute-start(f32[1,128,128]{2,1,0:T(8,128)S(1)} %get-tuple-element.23), channel_id=1, source_target_pairs={{0,32},{32,64},{64,96},{96,128},{128,160},{160,192},{192,224},{224... | collective-permute-start | bytes 196616 | tf_op jit(solution)/shard_map/ppermute | solution.py:26
  28.7 6.8 %collective-permute-start.1 = (f32[1,128,128]{2,1,0:T(8,128)S(1)}, f32[1,128,128]{2,1,0:T(8,128)S(1)}, u32[]{:S(2)}, u32[]{:S(2)}) collective-permute-start(f32[1,128,128]{2,1,0:T(8,128)S(1)} %slice.173), channel_id=1, source_target_pairs={{0,32},{32,64},{64,96},{96,128},{128,160},{160,192},{192,224},{224... | collective-permute-start | bytes 196616 | tf_op jit(solution)/shard_map/ppermute | solution.py:36
  35.5 1.9 %collective-permute-start = (f32[1,128,128]{2,1,0:T(8,128)S(1)}, f32[1,128,128]{2,1,0:T(8,128)S(1)}, u32[]{:S(2)}, u32[]{:S(2)}) collective-permute-start(f32[1,128,128]{2,1,0:T(8,128)S(1)} %slice.172), channel_id=1, source_target_pairs={{0,480},{32,0},{64,32},{96,64},{128,96},{160,128},{192,160},{224,1... | collective-permute-start | bytes 196616 | tf_op jit(solution)/shard_map/ppermute | solution.py:36
  37.5 1.9 %collective-permute-start.15 = (f32[1,128,128]{2,1,0:T(8,128)S(1)}, f32[1,128,128]{2,1,0:T(8,128)S(1)}, u32[]{:S(2)}, u32[]{:S(2)}) collective-permute-start(f32[1,128,128]{2,1,0:T(8,128)S(1)} %get-tuple-element.22), channel_id=1, source_target_pairs={{32,0},{64,32},{96,64},{128,96},{160,128},{192,160},{224,192},{256... | collective-permute-start | bytes 196616 | tf_op jit(solution)/shard_map/ppermute | solution.py:29
  39.4 6.4 %collective-permute-start.14 = (f32[1,128,128]{2,1,0:T(8,128)S(1)}, f32[1,128,128]{2,1,0:T(8,128)S(1)}, u32[]{:S(2)}, u32[]{:S(2)}) collective-permute-start(f32[1,128,128]{2,1,0:T(8,128)S(1)} %get-tuple-element.21), channel_id=1, source_target_pairs={{0,32},{32,64},{64,96},{96,128},{128,160},{160,192},{192,224},{224... | collective-permute-start | bytes 196616 | tf_op jit(solution)/shard_map/ppermute | solution.py:26
  46.3 5.8 %collective-permute-start.3 = (f32[1,128,128]{2,1,0:T(8,128)S(1)}, f32[1,128,128]{2,1,0:T(8,128)S(1)}, u32[]{:S(2)}, u32[]{:S(2)}) collective-permute-start(f32[1,128,128]{2,1,0:T(8,128)S(1)} %slice.177), channel_id=1, source_target_pairs={{0,32},{32,64},{64,96},{96,128},{128,160},{160,192},{192,224},{224... | collective-permute-start | bytes 196616 | tf_op jit(solution)/shard_map/ppermute | solution.py:36
  52.0 1.9 %collective-permute-start.2 = (f32[1,128,128]{2,1,0:T(8,128)S(1)}, f32[1,128,128]{2,1,0:T(8,128)S(1)}, u32[]{:S(2)}, u32[]{:S(2)}) collective-permute-start(f32[1,128,128]{2,1,0:T(8,128)S(1)} %slice.176), channel_id=1, source_target_pairs={{0,480},{32,0},{64,32},{96,64},{128,96},{160,128},{192,160},{224,1... | collective-permute-start | bytes 196616 | tf_op jit(solution)/shard_map/ppermute | solution.py:36
  56.7 6.3 %collective-permute-start.5 = (f32[1,128,128]{2,1,0:T(8,128)S(1)}, f32[1,128,128]{2,1,0:T(8,128)S(1)}, u32[]{:S(2)}, u32[]{:S(2)}) collective-permute-start(f32[1,128,128]{2,1,0:T(8,128)S(1)} %slice.181), channel_id=1, source_target_pairs={{0,32},{32,64},{64,96},{96,128},{128,160},{160,192},{192,224},{224... | collective-permute-start | bytes 196616 | tf_op jit(solution)/shard_map/ppermute | solution.py:36
  63.0 1.9 %collective-permute-start.4 = (f32[1,128,128]{2,1,0:T(8,128)S(1)}, f32[1,128,128]{2,1,0:T(8,128)S(1)}, u32[]{:S(2)}, u32[]{:S(2)}) collective-permute-start(f32[1,128,128]{2,1,0:T(8,128)S(1)} %slice.180), channel_id=1, source_target_pairs={{0,480},{32,0},{64,32},{96,64},{128,96},{160,128},{192,160},{224,1... | collective-permute-start | bytes 196616 | tf_op jit(solution)/shard_map/ppermute | solution.py:36
  65.0 1.8 collective-permute-done.4
  67.6 5.8 %collective-permute-start.7 = (f32[1,128,128]{2,1,0:T(8,128)S(1)}, f32[1,128,128]{2,1,0:T(8,128)S(1)}, u32[]{:S(2)}, u32[]{:S(2)}) collective-permute-start(f32[1,128,128]{2,1,0:T(8,128)S(1)} %slice.185), channel_id=1, source_target_pairs={{0,32},{32,64},{64,96},{96,128},{128,160},{160,192},{192,224},{224... | collective-permute-start | bytes 196616 | tf_op jit(solution)/shard_map/ppermute | solution.py:36
  73.4 1.9 %collective-permute-start.6 = (f32[1,128,128]{2,1,0:T(8,128)S(1)}, f32[1,128,128]{2,1,0:T(8,128)}, u32[]{:S(2)}, u32[]{:S(2)}) collective-permute-start(f32[1,128,128]{2,1,0:T(8,128)S(1)} %slice.184), channel_id=1, source_target_pairs={{0,480},{32,0},{64,32},{96,64},{128,96},{160,128},{192,160},{224,1... | collective-permute-start | bytes 196616 | tf_op jit(solution)/shard_map/ppermute | solution.py:36
  76.1 17.9 %all-to-all-start.3 = ((f32[32,16,1]{1,2,0:T(1,128)}), f32[32,16,1]{1,2,0:T(1,128)S(1)}, u32[]{:S(2)}, u32[]{:S(2)}) async-start(f32[32,16,1]{1,2,0:T(1,128)} %bitcast.29), calls=%async_computation.3 | async-start | bytes 32768 | tf_op jit(solution)/shard_map/all_to_all | solution.py:144
  94.1 14.7 %all-to-all-done.3 = f32[32,16,1]{1,2,0:T(1,128)S(1)} async-done(((f32[32,16,1]{1,2,0:T(1,128)}), f32[32,16,1]{1,2,0:T(1,128)S(1)}, u32[]{:S(2)}, u32[]{:S(2)}) %all-to-all-start.3) | async-done | bytes 2080 | tf_op jit(solution)/shard_map/all_to_all | solution.py:144
  108.8 3.9 %all-to-all-start.2 = ((bf16[32,16,128]{2,1,0:T(8,128)(2,1)}), bf16[32,16,128]{2,1,0:T(8,128)(2,1)S(1)}, u32[]{:S(2)}, u32[]{:S(2)}) async-start(bf16[32,16,128]{2,1,0:T(8,128)(2,1)} %bitcast.21), calls=%async_computation.2 | async-start | bytes 262144 | tf_op jit(solution)/shard_map/all_to_all | solution.py:146
  114.8 15.6 %all-to-all-done.2 = bf16[32,16,128]{2,1,0:T(8,128)(2,1)S(1)} async-done(((bf16[32,16,128]{2,1,0:T(8,128)(2,1)}), bf16[32,16,128]{2,1,0:T(8,128)(2,1)S(1)}, u32[]{:S(2)}, u32[]{:S(2)}) %all-to-all-start.2) | async-done | bytes 131104 | tf_op jit(solution)/shard_map/all_to_all | solution.py:146
  130.5 4.1 %all-to-all-start = ((f32[32,16,128]{2,1,0:T(8,128)}), f32[32,16,128]{2,1,0:T(8,128)S(1)}, u32[]{:S(2)}, u32[]{:S(2)}) async-start(f32[32,16,128]{2,1,0:T(8,128)} %bitcast.13), calls=%async_computation | async-start | bytes 524288 | tf_op jit(solution)/shard_map/all_to_all | solution.py:143
  134.6 3.6 %stack.10 = f32[9,13824]{1,0:T(8,128)} concatenate(f32[1,13824]{1,0:T(1,128)} %get-tuple-element.33, f32[1,13824]{1,0:T(1,128)S(1)} %get-tuple-element.32, f32[1,13824]{1,0:T(1,128)S(1)} %get-tuple-element.31, f32[1,13824]{1,0:T(1,128)S(1)} %get-tuple-element.32, f32[1,13824]{1,0:T(1,128)S(1)} %get-tuple-element.30, f32[1,13824]{1,0:T(1,128)S(1)} %get-tuple-element.29, ...), dimensions={0} | concatenate | bytes 995328 | tf_op jit(solution)/shard_map/stack | solution.py:62
  139.9 1.8 mul.3480
  143.1 13.5 %all-to-all-done = f32[32,16,128]{2,1,0:T(8,128)S(1)} async-done(((f32[32,16,128]{2,1,0:T(8,128)}), f32[32,16,128]{2,1,0:T(8,128)S(1)}, u32[]{:S(2)}, u32[]{:S(2)}) %all-to-all-start) | async-done | bytes 262176 | tf_op jit(solution)/shard_map/all_to_all | solution.py:143
  156.8 1.9 fusion.5
  159.9 2.2 %fusion.2 = f32[16,13824]{1,0:T(8,128)S(1)} fusion(f32[16,13824]{1,0:T(8,128)S(1)} %mul.3484, f32[9,13824]{1,0:T(8,128)} %stack.10, f32[9,16]{1,0:T(8,128)S(1)} %copy-done), kind=kOutput, calls=%fused_computation.3 | convolution fusion | flops 24551424 | bytes 2267712 | tf_op jit(solution)/shard_map/sc,sq->cq/dot_general | solution.py:153
  164.9 3.9 %all-to-all-start.1 = ((f32[16,32,128]{2,0,1:T(8,128)}), f32[16,32,128]{2,0,1:T(8,128)S(1)}, u32[]{:S(2)}, u32[]{:S(2)}) async-start(f32[16,32,128]{2,0,1:T(8,128)} %copy.17), calls=%async_computation.1 | async-start | bytes 524288 | tf_op jit(solution)/shard_map/all_to_all | solution.py:162
  170.9 2.2 %convolution_multiply_fusion.2 = f32[6,16]{1,0:T(8,128)S(1)} fusion(f32[6,13824]{1,0:T(8,128)} %stack.11, f32[16,13824]{1,0:T(8,128)S(1)} %mul.3484, f32[16,13824]{1,0:T(8,128)S(1)} %reshape.613), kind=kOutput, calls=%fused_computation.9 | convolution fusion | flops 16146528 | bytes 2101632 | tf_op jit(solution)/shard_map/pq,cq->pc/dot_general | solution.py:159
  173.1 2.0 %stack.12 = f32[9,16]{1,0:T(8,128)} concatenate(f32[3,16]{1,0:T(4,128)S(1)} %slice.148, f32[1,16]{1,0:T(1,128)S(1)} %get-tuple-element.38, f32[2,16]{1,0:T(2,128)S(1)} %get-tuple-element.36, f32[1,16]{1,0:T(1,128)S(1)} %get-tuple-element.37, f32[2,16]{1,0:T(2,128)S(1)} %get-tuple-element.35), dimensions={0} | concatenate | bytes 1152 | tf_op jit(solution)/shard_map/stack | solution.py:163
  175.1 14.8 %all-to-all-done.1 = f32[16,32,128]{2,0,1:T(8,128)S(1)} async-done(((f32[16,32,128]{2,0,1:T(8,128)}), f32[16,32,128]{2,0,1:T(8,128)S(1)}, u32[]{:S(2)}, u32[]{:S(2)}) %all-to-all-start.1) | async-done | bytes 262176 | tf_op jit(solution)/shard_map/all_to_all | solution.py:162
  (132 shorter events, 24.9 us)
Async XLA Ops:
  0.6 159.3 %copy-start = (f32[9,16]{1,0:T(8,128)S(1)}, f32[9,16]{1,0:T(8,128)}, u32[]{:S(2)}) copy-start(f32[9,16]{1,0:T(8,128)} %param.11) | copy-start | bytes 1732
  1.7 9.1 %collective-permute-start.9 = (f32[1,128,128]{2,1,0:T(8,128)S(1)}, f32[1,128,128]{2,1,0:T(8,128)S(1)}, u32[]{:S(2)}, u32[]{:S(2)}) collective-permute-start(f32[1,128,128]{2,1,0:T(8,128)S(1)} %get-tuple-element.28), channel_id=1, source_target_pairs={{32,0},{64,32},{96,64},{128,96},{160,128},{192,160},{224,192},{256... | collective-permute-start | bytes 196616 | tf_op jit(solution)/shard_map/ppermute | solution.py:29
  3.8 7.0 %collective-permute-start.8 = (f32[1,128,128]{2,1,0:T(8,128)S(1)}, f32[1,128,128]{2,1,0:T(8,128)S(1)}, u32[]{:S(2)}, u32[]{:S(2)}) collective-permute-start(f32[1,128,128]{2,1,0:T(8,128)S(1)} %get-tuple-element.27), channel_id=1, source_target_pairs={{0,32},{32,64},{64,96},{96,128},{128,160},{160,192},{192,224},{224... | collective-permute-start | bytes 196616 | tf_op jit(solution)/shard_map/ppermute | solution.py:26
  7.6 20.7 %copy-start.2 = (f32[512,128]{1,0:T(8,128)S(1)}, f32[512,128]{1,0:T(8,128)}, u32[]{:S(2)}) copy-start(f32[512,128]{1,0:T(8,128)} %param.6) | copy-start | bytes 786436
  7.6 20.7 %copy-start.7 = (f32[512]{0:T(512)S(1)}, f32[512]{0:T(512)}, u32[]{:S(2)}) copy-start(f32[512]{0:T(512)} %param.9) | copy-start | bytes 6148
  11.1 7.6 %collective-permute-start.11 = (f32[1,128,128]{2,1,0:T(8,128)S(1)}, f32[1,128,128]{2,1,0:T(8,128)S(1)}, u32[]{:S(2)}, u32[]{:S(2)}) collective-permute-start(f32[1,128,128]{2,1,0:T(8,128)S(1)} %get-tuple-element.26), channel_id=1, source_target_pairs={{32,0},{64,32},{96,64},{128,96},{160,128},{192,160},{224,192},{256... | collective-permute-start | bytes 196616 | tf_op jit(solution)/shard_map/ppermute | solution.py:29
  14.4 5.6 %collective-permute-start.10 = (f32[1,128,128]{2,1,0:T(8,128)S(1)}, f32[1,128,128]{2,1,0:T(8,128)S(1)}, u32[]{:S(2)}, u32[]{:S(2)}) collective-permute-start(f32[1,128,128]{2,1,0:T(8,128)S(1)} %get-tuple-element.25), channel_id=1, source_target_pairs={{0,32},{32,64},{64,96},{96,128},{128,160},{160,192},{192,224},{224... | collective-permute-start | bytes 196616 | tf_op jit(solution)/shard_map/ppermute | solution.py:26
  20.3 7.7 %collective-permute-start.13 = (f32[1,128,128]{2,1,0:T(8,128)S(1)}, f32[1,128,128]{2,1,0:T(8,128)S(1)}, u32[]{:S(2)}, u32[]{:S(2)}) collective-permute-start(f32[1,128,128]{2,1,0:T(8,128)S(1)} %get-tuple-element.24), channel_id=1, source_target_pairs={{32,0},{64,32},{96,64},{128,96},{160,128},{192,160},{224,192},{256... | collective-permute-start | bytes 196616 | tf_op jit(solution)/shard_map/ppermute | solution.py:29
  22.2 6.1 %collective-permute-start.12 = (f32[1,128,128]{2,1,0:T(8,128)S(1)}, f32[1,128,128]{2,1,0:T(8,128)S(1)}, u32[]{:S(2)}, u32[]{:S(2)}) collective-permute-start(f32[1,128,128]{2,1,0:T(8,128)S(1)} %get-tuple-element.23), channel_id=1, source_target_pairs={{0,32},{32,64},{64,96},{96,128},{128,160},{160,192},{192,224},{224... | collective-permute-start | bytes 196616 | tf_op jit(solution)/shard_map/ppermute | solution.py:26
  28.7 17.1 %collective-permute-start.1 = (f32[1,128,128]{2,1,0:T(8,128)S(1)}, f32[1,128,128]{2,1,0:T(8,128)S(1)}, u32[]{:S(2)}, u32[]{:S(2)}) collective-permute-start(f32[1,128,128]{2,1,0:T(8,128)S(1)} %slice.173), channel_id=1, source_target_pairs={{0,32},{32,64},{64,96},{96,128},{128,160},{160,192},{192,224},{224... | collective-permute-start | bytes 196616 | tf_op jit(solution)/shard_map/ppermute | solution.py:36
  35.5 10.3 %collective-permute-start = (f32[1,128,128]{2,1,0:T(8,128)S(1)}, f32[1,128,128]{2,1,0:T(8,128)S(1)}, u32[]{:S(2)}, u32[]{:S(2)}) collective-permute-start(f32[1,128,128]{2,1,0:T(8,128)S(1)} %slice.172), channel_id=1, source_target_pairs={{0,480},{32,0},{64,32},{96,64},{128,96},{160,128},{192,160},{224,1... | collective-permute-start | bytes 196616 | tf_op jit(solution)/shard_map/ppermute | solution.py:36
  37.5 17.1 %collective-permute-start.15 = (f32[1,128,128]{2,1,0:T(8,128)S(1)}, f32[1,128,128]{2,1,0:T(8,128)S(1)}, u32[]{:S(2)}, u32[]{:S(2)}) collective-permute-start(f32[1,128,128]{2,1,0:T(8,128)S(1)} %get-tuple-element.22), channel_id=1, source_target_pairs={{32,0},{64,32},{96,64},{128,96},{160,128},{192,160},{224,192},{256... | collective-permute-start | bytes 196616 | tf_op jit(solution)/shard_map/ppermute | solution.py:29
  39.4 15.2 %collective-permute-start.14 = (f32[1,128,128]{2,1,0:T(8,128)S(1)}, f32[1,128,128]{2,1,0:T(8,128)S(1)}, u32[]{:S(2)}, u32[]{:S(2)}) collective-permute-start(f32[1,128,128]{2,1,0:T(8,128)S(1)} %get-tuple-element.21), channel_id=1, source_target_pairs={{0,32},{32,64},{64,96},{96,128},{128,160},{160,192},{192,224},{224... | collective-permute-start | bytes 196616 | tf_op jit(solution)/shard_map/ppermute | solution.py:26
  46.3 8.4 %collective-permute-start.3 = (f32[1,128,128]{2,1,0:T(8,128)S(1)}, f32[1,128,128]{2,1,0:T(8,128)S(1)}, u32[]{:S(2)}, u32[]{:S(2)}) collective-permute-start(f32[1,128,128]{2,1,0:T(8,128)S(1)} %slice.177), channel_id=1, source_target_pairs={{0,32},{32,64},{64,96},{96,128},{128,160},{160,192},{192,224},{224... | collective-permute-start | bytes 196616 | tf_op jit(solution)/shard_map/ppermute | solution.py:36
  52.0 3.8 %collective-permute-start.2 = (f32[1,128,128]{2,1,0:T(8,128)S(1)}, f32[1,128,128]{2,1,0:T(8,128)S(1)}, u32[]{:S(2)}, u32[]{:S(2)}) collective-permute-start(f32[1,128,128]{2,1,0:T(8,128)S(1)} %slice.176), channel_id=1, source_target_pairs={{0,480},{32,0},{64,32},{96,64},{128,96},{160,128},{192,160},{224,1... | collective-permute-start | bytes 196616 | tf_op jit(solution)/shard_map/ppermute | solution.py:36
  56.7 8.3 %collective-permute-start.5 = (f32[1,128,128]{2,1,0:T(8,128)S(1)}, f32[1,128,128]{2,1,0:T(8,128)S(1)}, u32[]{:S(2)}, u32[]{:S(2)}) collective-permute-start(f32[1,128,128]{2,1,0:T(8,128)S(1)} %slice.181), channel_id=1, source_target_pairs={{0,32},{32,64},{64,96},{96,128},{128,160},{160,192},{192,224},{224... | collective-permute-start | bytes 196616 | tf_op jit(solution)/shard_map/ppermute | solution.py:36
  63.0 3.8 %collective-permute-start.4 = (f32[1,128,128]{2,1,0:T(8,128)S(1)}, f32[1,128,128]{2,1,0:T(8,128)S(1)}, u32[]{:S(2)}, u32[]{:S(2)}) collective-permute-start(f32[1,128,128]{2,1,0:T(8,128)S(1)} %slice.180), channel_id=1, source_target_pairs={{0,480},{32,0},{64,32},{96,64},{128,96},{160,128},{192,160},{224,1... | collective-permute-start | bytes 196616 | tf_op jit(solution)/shard_map/ppermute | solution.py:36
  67.6 45.1 %collective-permute-start.7 = (f32[1,128,128]{2,1,0:T(8,128)S(1)}, f32[1,128,128]{2,1,0:T(8,128)S(1)}, u32[]{:S(2)}, u32[]{:S(2)}) collective-permute-start(f32[1,128,128]{2,1,0:T(8,128)S(1)} %slice.185), channel_id=1, source_target_pairs={{0,32},{32,64},{64,96},{96,128},{128,160},{160,192},{192,224},{224... | collective-permute-start | bytes 196616 | tf_op jit(solution)/shard_map/ppermute | solution.py:36
  73.4 39.3 %collective-permute-start.6 = (f32[1,128,128]{2,1,0:T(8,128)S(1)}, f32[1,128,128]{2,1,0:T(8,128)}, u32[]{:S(2)}, u32[]{:S(2)}) collective-permute-start(f32[1,128,128]{2,1,0:T(8,128)S(1)} %slice.184), channel_id=1, source_target_pairs={{0,480},{32,0},{64,32},{96,64},{128,96},{160,128},{192,160},{224,1... | collective-permute-start | bytes 196616 | tf_op jit(solution)/shard_map/ppermute | solution.py:36
  76.1 32.7 %all-to-all-start.3 = ((f32[32,16,1]{1,2,0:T(1,128)}), f32[32,16,1]{1,2,0:T(1,128)S(1)}, u32[]{:S(2)}, u32[]{:S(2)}) async-start(f32[32,16,1]{1,2,0:T(1,128)} %bitcast.29), calls=%async_computation.3 | async-start | bytes 32768 | tf_op jit(solution)/shard_map/all_to_all | solution.py:144
  94.1 44.1 %copy-start.4 = (f32[1,13824]{1,0:T(1,128)S(1)}, f32[1,13824]{1,0:T(1,128)}, u32[]{:S(2)}) copy-start(f32[1,13824]{1,0:T(1,128)} %get-tuple-element.33) | copy-start | bytes 165892
  94.1 44.1 %copy-start.5 = (f32[1,13824]{1,0:T(1,128)S(1)}, f32[1,13824]{1,0:T(1,128)}, u32[]{:S(2)}) copy-start(f32[1,13824]{1,0:T(1,128)} %get-tuple-element.9) | copy-start | bytes 165892
  108.8 21.7 %copy-start.6 = (f32[32,16,1]{1,2,0:T(1,128)}, f32[32,16,1]{1,2,0:T(1,128)S(1)}, u32[]{:S(2)}) copy-start(f32[32,16,1]{1,2,0:T(1,128)S(1)} %all-to-all-done.3) | copy-start | bytes 6148
  108.8 21.7 %all-to-all-start.2 = ((bf16[32,16,128]{2,1,0:T(8,128)(2,1)}), bf16[32,16,128]{2,1,0:T(8,128)(2,1)S(1)}, u32[]{:S(2)}, u32[]{:S(2)}) async-start(bf16[32,16,128]{2,1,0:T(8,128)(2,1)} %bitcast.21), calls=%async_computation.2 | async-start | bytes 262144 | tf_op jit(solution)/shard_map/all_to_all | solution.py:146
  112.7 26.8 %copy-start.9 = (f32[1,24]{1,0:T(1,128)S(1)}, f32[1,24]{1,0:T(1,128)}, u32[]{:S(2)}) copy-start(f32[1,24]{1,0:T(1,128)} %get-tuple-element.69) | copy-start | bytes 292
  112.7 26.8 %copy-start.10 = (f32[1,24]{1,0:T(1,128)S(1)}, f32[1,24]{1,0:T(1,128)}, u32[]{:S(2)}) copy-start(f32[1,24]{1,0:T(1,128)} %get-tuple-element.70) | copy-start | bytes 292
  112.7 26.8 %copy-start.11 = (f32[1,24]{1,0:T(1,128)S(1)}, f32[1,24]{1,0:T(1,128)}, u32[]{:S(2)}) copy-start(f32[1,24]{1,0:T(1,128)} %get-tuple-element.67) | copy-start | bytes 292
  112.7 26.8 %copy-start.12 = (f32[1,24]{1,0:T(1,128)S(1)}, f32[1,24]{1,0:T(1,128)}, u32[]{:S(2)}) copy-start(f32[1,24]{1,0:T(1,128)} %get-tuple-element.68) | copy-start | bytes 292
  112.7 26.8 %copy-start.13 = (f32[1,24]{1,0:T(1,128)S(1)}, f32[1,24]{1,0:T(1,128)}, u32[]{:S(2)}) copy-start(f32[1,24]{1,0:T(1,128)} %get-tuple-element.65) | copy-start | bytes 292
  112.7 26.8 %copy-start.14 = (f32[1,24]{1,0:T(1,128)S(1)}, f32[1,24]{1,0:T(1,128)}, u32[]{:S(2)}) copy-start(f32[1,24]{1,0:T(1,128)} %get-tuple-element.66) | copy-start | bytes 292
  130.5 26.1 %all-to-all-start = ((f32[32,16,128]{2,1,0:T(8,128)}), f32[32,16,128]{2,1,0:T(8,128)S(1)}, u32[]{:S(2)}, u32[]{:S(2)}) async-start(f32[32,16,128]{2,1,0:T(8,128)} %bitcast.13), calls=%async_computation | async-start | bytes 524288 | tf_op jit(solution)/shard_map/all_to_all | solution.py:143
  164.9 25.1 %all-to-all-start.1 = ((f32[16,32,128]{2,0,1:T(8,128)}), f32[16,32,128]{2,0,1:T(8,128)S(1)}, u32[]{:S(2)}, u32[]{:S(2)}) async-start(f32[16,32,128]{2,0,1:T(8,128)} %copy.17), calls=%async_computation.1 | async-start | bytes 524288 | tf_op jit(solution)/shard_map/all_to_all | solution.py:162
  (3 other events, 32.7 us)
where the time goes:
time: 192 us; the launch traced here: 191 us
  starting transfers between devices  88.8 us (46%)
  waiting for transfers between devices  63.4 us (33%)
  local copies, waits for them, and re-layouts  14 us (7%)
  other arithmetic  12.6 us (7%)
  matrix products  10.4 us (5%)
    ppermute x8, starting transfers between devices, shifted(): lax.ppermute(shard, axis, [(i, (i + by) % count) for i in range(count)])  32.3 us
    all_to_all x1, starting transfers between devices, body(): lax.all_to_all(speed_column, 'coef', split_axis=0, concat_axis=1, tiled=T...  17.9 us
    ppermute x4, starting transfers between devices, extended(): lax.ppermute(lax.slice_in_dim(block, block.shape[dim] - width, None, axis...  17.5 us
    all_to_all x1, waiting for transfers between devices, body(): lax.all_to_all(source_state, 'coef', split_axis=0, concat_axis=1, tiled=T...  15.6 us
    all_to_all x1, waiting for transfers between devices, body(): lax.all_to_all(adj_cells, 'coef', split_axis=1, concat_axis=0, tiled=True)  14.8 us
    all_to_all x1, waiting for transfers between devices, body(): lax.all_to_all(speed_column, 'coef', split_axis=0, concat_axis=1, tiled=T...  14.7 us
    all_to_all x1, waiting for transfers between devices, body(): lax.all_to_all(mu_field, 'coef', split_axis=0, concat_axis=1, tiled=True)  13.5 us
    ppermute x4, starting transfers between devices, extended(): lax.ppermute(lax.slice_in_dim(block, 0, width, axis=dim), axis, backward)  9.26 us
  transfers between devices with their start and end apart: 20, of which 8 were waited for; matrix products, arithmetic and copies ran while one was open for 13% of the time, Pallas kernels for 0%

commit v1 on v0

--- a/solution.py
+++ b/solution.py
@@ -159,7 +159,12 @@
     strain_unique = time_step * jnp.einsum(
         "pq,cq->pc", unique_table, adj_values * source_values, precision=highest
     )
-    adj_source = lax.all_to_all(adj_cells, "coef", split_axis=1, concat_axis=0, tiled=True)
+    adj_source = jnp.concatenate(
+        lax.all_to_all(
+            jnp.stack(jnp.split(adj_cells, lax.axis_size("coef"), axis=1)), "coef", 0, 0
+        ),
+        axis=0,
+    )
     adj_strain = jnp.stack([strain_unique[slot_no] for slot_no in pair_slots])
     return (adj_source, adj_strain, adj_courant)
 

time: 192 us -> 210 us (1.094)
  local copies, waits for them, and re-layouts: 14 us -> 32.4 us
    unnamed x31 -> x62, local copies, waits for them, and re-layouts: 0.78 us -> 19.4 us
  transfers between devices with their start and end apart: 20 -> 20, of which waited for: 8 -> 8; matrix products, arithmetic and copies ran while one was open for 13% -> 12% of each run, Pallas kernels for 0% -> 0%
where the time goes in v1:
time: 210 us; the launch traced here: 209 us
  starting transfers between devices  88.8 us (42%)
  waiting for transfers between devices  63.4 us (30%)
  local copies, waits for them, and re-layouts  32.4 us (15%)
  other arithmetic  12.6 us (6%)
  matrix products  10.4 us (5%)
    ppermute x8, starting transfers between devices, shifted(): lax.ppermute(shard, axis, [(i, (i + by) % count) for i in range(count)])  32.3 us
    unnamed x62, local copies, waits for them, and re-layouts  19.4 us
    all_to_all x1, starting transfers between devices, body(): lax.all_to_all(speed_column, 'coef', split_axis=0, concat_axis=1, tiled=T...  17.9 us
    ppermute x4, starting transfers between devices, extended(): lax.ppermute(lax.slice_in_dim(block, block.shape[dim] - width, None, axis...  17.5 us
    all_to_all x1, waiting for transfers between devices, body(): lax.all_to_all(source_state, 'coef', split_axis=0, concat_axis=1, tiled=T...  15.6 us
    all_to_all x1, waiting for transfers between devices, body(): lax.all_to_all(jnp.stack(jnp.split(adj_cells, lax.axis_size('coef'), axis...  14.8 us
    all_to_all x1, waiting for transfers between devices, body(): lax.all_to_all(speed_column, 'coef', split_axis=0, concat_axis=1, tiled=T...  14.7 us
    all_to_all x1, waiting for transfers between devices, body(): lax.all_to_all(mu_field, 'coef', split_axis=0, concat_axis=1, tiled=True)  13.5 us
  transfers between devices with their start and end apart: 20, of which 8 were waited for; matrix products, arithmetic and copies ran while one was open for 12% of the time, Pallas kernels for 0%

profile of v1, /device:TPU:24, one launch (start us, length us, event | category | flops | bytes accessed | tf_op | source)
XLA Modules:
  0.0 209.0 jit_solution(12393909474459514668)
XLA Ops:
  1.7 2.1 %collective-permute-start.9 = (f32[1,128,128]{2,1,0:T(8,128)S(1)}, f32[1,128,128]{2,1,0:T(8,128)S(1)}, u32[]{:S(2)}, u32[]{:S(2)}) collective-permute-start(f32[1,128,128]{2,1,0:T(8,128)S(1)} %get-tuple-element.28), channel_id=1, source_target_pairs={{32,0},{64,32},{96,64},{128,96},{160,128},{192,160},{224,192},{256... | collective-permute-start | bytes 196616 | tf_op jit(solution)/shard_map/ppermute | solution.py:29
  3.8 2.2 %collective-permute-start.8 = (f32[1,128,128]{2,1,0:T(8,128)S(1)}, f32[1,128,128]{2,1,0:T(8,128)S(1)}, u32[]{:S(2)}, u32[]{:S(2)}) collective-permute-start(f32[1,128,128]{2,1,0:T(8,128)S(1)} %get-tuple-element.27), channel_id=1, source_target_pairs={{0,32},{32,64},{64,96},{96,128},{128,160},{160,192},{192,224},{224... | collective-permute-start | bytes 196616 | tf_op jit(solution)/shard_map/ppermute | solution.py:26
  11.1 3.3 %collective-permute-start.11 = (f32[1,128,128]{2,1,0:T(8,128)S(1)}, f32[1,128,128]{2,1,0:T(8,128)S(1)}, u32[]{:S(2)}, u32[]{:S(2)}) collective-permute-start(f32[1,128,128]{2,1,0:T(8,128)S(1)} %get-tuple-element.26), channel_id=1, source_target_pairs={{32,0},{64,32},{96,64},{128,96},{160,128},{192,160},{224,192},{256... | collective-permute-start | bytes 196616 | tf_op jit(solution)/shard_map/ppermute | solution.py:29
  14.4 3.7 %collective-permute-start.10 = (f32[1,128,128]{2,1,0:T(8,128)S(1)}, f32[1,128,128]{2,1,0:T(8,128)S(1)}, u32[]{:S(2)}, u32[]{:S(2)}) collective-permute-start(f32[1,128,128]{2,1,0:T(8,128)S(1)} %get-tuple-element.25), channel_id=1, source_target_pairs={{0,32},{32,64},{64,96},{96,128},{128,160},{160,192},{192,224},{224... | collective-permute-start | bytes 196616 | tf_op jit(solution)/shard_map/ppermute | solution.py:26
  18.7 1.4 collective-permute-done.10
  20.3 1.9 collective-permute-start.13
  22.2 5.2 %collective-permute-start.12 = (f32[1,128,128]{2,1,0:T(8,128)S(1)}, f32[1,128,128]{2,1,0:T(8,128)S(1)}, u32[]{:S(2)}, u32[]{:S(2)}) collective-permute-start(f32[1,128,128]{2,1,0:T(8,128)S(1)} %get-tuple-element.23), channel_id=1, source_target_pairs={{0,32},{32,64},{64,96},{96,128},{128,160},{160,192},{192,224},{224... | collective-permute-start | bytes 196616 | tf_op jit(solution)/shard_map/ppermute | solution.py:26
  28.7 6.8 %collective-permute-start.1 = (f32[1,128,128]{2,1,0:T(8,128)S(1)}, f32[1,128,128]{2,1,0:T(8,128)S(1)}, u32[]{:S(2)}, u32[]{:S(2)}) collective-permute-start(f32[1,128,128]{2,1,0:T(8,128)S(1)} %slice.173), channel_id=1, source_target_pairs={{0,32},{32,64},{64,96},{96,128},{128,160},{160,192},{192,224},{224... | collective-permute-start | bytes 196616 | tf_op jit(solution)/shard_map/ppermute | solution.py:36
  35.5 1.9 collective-permute-start
  37.5 1.9 collective-permute-start.15
  39.4 6.4 %collective-permute-start.14 = (f32[1,128,128]{2,1,0:T(8,128)S(1)}, f32[1,128,128]{2,1,0:T(8,128)S(1)}, u32[]{:S(2)}, u32[]{:S(2)}) collective-permute-start(f32[1,128,128]{2,1,0:T(8,128)S(1)} %get-tuple-element.21), channel_id=1, source_target_pairs={{0,32},{32,64},{64,96},{96,128},{128,160},{160,192},{192,224},{224... | collective-permute-start | bytes 196616 | tf_op jit(solution)/shard_map/ppermute | solution.py:26
  46.3 5.8 %collective-permute-start.3 = (f32[1,128,128]{2,1,0:T(8,128)S(1)}, f32[1,128,128]{2,1,0:T(8,128)S(1)}, u32[]{:S(2)}, u32[]{:S(2)}) collective-permute-start(f32[1,128,128]{2,1,0:T(8,128)S(1)} %slice.177), channel_id=1, source_target_pairs={{0,32},{32,64},{64,96},{96,128},{128,160},{160,192},{192,224},{224... | collective-permute-start | bytes 196616 | tf_op jit(solution)/shard_map/ppermute | solution.py:36
  52.0 1.9 collective-permute-start.2
  56.7 6.3 %collective-permute-start.5 = (f32[1,128,128]{2,1,0:T(8,128)S(1)}, f32[1,128,128]{2,1,0:T(8,128)S(1)}, u32[]{:S(2)}, u32[]{:S(2)}) collective-permute-start(f32[1,128,128]{2,1,0:T(8,128)S(1)} %slice.181), channel_id=1, source_target_pairs={{0,32},{32,64},{64,96},{96,128},{128,160},{160,192},{192,224},{224... | collective-permute-start | bytes 196616 | tf_op jit(solution)/shard_map/ppermute | solution.py:36
  63.0 1.9 collective-permute-start.4
  65.0 1.8 collective-permute-done.4
  67.6 5.8 %collective-permute-start.7 = (f32[1,128,128]{2,1,0:T(8,128)S(1)}, f32[1,128,128]{2,1,0:T(8,128)S(1)}, u32[]{:S(2)}, u32[]{:S(2)}) collective-permute-start(f32[1,128,128]{2,1,0:T(8,128)S(1)} %slice.185), channel_id=1, source_target_pairs={{0,32},{32,64},{64,96},{96,128},{128,160},{160,192},{192,224},{224... | collective-permute-start | bytes 196616 | tf_op jit(solution)/shard_map/ppermute | solution.py:36
  73.4 1.9 collective-permute-start.6
  76.1 17.9 %all-to-all-start.3 = ((f32[32,16,1]{1,2,0:T(1,128)}), f32[32,16,1]{1,2,0:T(1,128)S(1)}, u32[]{:S(2)}, u32[]{:S(2)}) async-start(f32[32,16,1]{1,2,0:T(1,128)} %bitcast.60), calls=%async_computation.3 | async-start | bytes 32768 | tf_op jit(solution)/shard_map/all_to_all | solution.py:144
  94.1 14.7 %all-to-all-done.3 = f32[32,16,1]{1,2,0:T(1,128)S(1)} async-done(((f32[32,16,1]{1,2,0:T(1,128)}), f32[32,16,1]{1,2,0:T(1,128)S(1)}, u32[]{:S(2)}, u32[]{:S(2)}) %all-to-all-start.3) | async-done | bytes 2080 | tf_op jit(solution)/shard_map/all_to_all | solution.py:144
  108.8 3.9 %all-to-all-start.2 = ((bf16[32,16,128]{2,1,0:T(8,128)(2,1)}), bf16[32,16,128]{2,1,0:T(8,128)(2,1)S(1)}, u32[]{:S(2)}, u32[]{:S(2)}) async-start(bf16[32,16,128]{2,1,0:T(8,128)(2,1)} %bitcast.52), calls=%async_computation.2 | async-start | bytes 262144 | tf_op jit(solution)/shard_map/all_to_all | solution.py:146
  114.8 15.6 %all-to-all-done.2 = bf16[32,16,128]{2,1,0:T(8,128)(2,1)S(1)} async-done(((bf16[32,16,128]{2,1,0:T(8,128)(2,1)}), bf16[32,16,128]{2,1,0:T(8,128)(2,1)S(1)}, u32[]{:S(2)}, u32[]{:S(2)}) %all-to-all-start.2) | async-done | bytes 131104 | tf_op jit(solution)/shard_map/all_to_all | solution.py:146
  130.5 4.1 %all-to-all-start = ((f32[32,16,128]{2,1,0:T(8,128)}), f32[32,16,128]{2,1,0:T(8,128)S(1)}, u32[]{:S(2)}, u32[]{:S(2)}) async-start(f32[32,16,128]{2,1,0:T(8,128)} %bitcast.13), calls=%async_computation | async-start | bytes 524288 | tf_op jit(solution)/shard_map/all_to_all | solution.py:143
  134.6 3.6 %stack.138 = f32[9,13824]{1,0:T(8,128)} concatenate(f32[1,13824]{1,0:T(1,128)} %get-tuple-element.33, f32[1,13824]{1,0:T(1,128)S(1)} %get-tuple-element.32, f32[1,13824]{1,0:T(1,128)S(1)} %get-tuple-element.31, f32[1,13824]{1,0:T(1,128)S(1)} %get-tuple-element.32, f32[1,13824]{1,0:T(1,128)S(1)} %get-tuple-element.30, f32[1,13824]{1,0:T(1,128)S(1)} %get-tuple-element.29, ...), dimensions={0} | concatenate | bytes 995328 | tf_op jit(solution)/shard_map/stack | solution.py:62
  139.9 1.8 mul.3480
  143.1 13.5 %all-to-all-done = f32[32,16,128]{2,1,0:T(8,128)S(1)} async-done(((f32[32,16,128]{2,1,0:T(8,128)}), f32[32,16,128]{2,1,0:T(8,128)S(1)}, u32[]{:S(2)}, u32[]{:S(2)}) %all-to-all-start) | async-done | bytes 262176 | tf_op jit(solution)/shard_map/all_to_all | solution.py:143
  156.8 1.9 fusion.5
  159.9 2.2 %fusion.2 = f32[16,13824]{1,0:T(8,128)S(1)} fusion(f32[16,13824]{1,0:T(8,128)S(1)} %mul.3484, f32[9,13824]{1,0:T(8,128)} %stack.138, f32[9,16]{1,0:T(8,128)S(1)} %copy-done), kind=kOutput, calls=%fused_computation.3 | convolution fusion | flops 24551424 | bytes 2267712 | tf_op jit(solution)/shard_map/sc,sq->cq/dot_general | solution.py:153
  183.2 3.9 %all-to-all-start.1 = ((f32[32,16,128]{2,1,0:T(8,128)}), f32[32,16,128]{2,1,0:T(8,128)S(1)}, u32[]{:S(2)}, u32[]{:S(2)}) async-start(f32[32,16,128]{2,1,0:T(8,128)} %constant_dynamic-update-slice_fusion), calls=%async_computation.1 | async-start | bytes 524288 | tf_op jit(solution)/shard_map/all_to_all | solution.py:163
  189.3 2.2 %convolution_multiply_fusion.2 = f32[6,16]{1,0:T(8,128)S(1)} fusion(f32[6,13824]{1,0:T(8,128)} %stack.172, f32[16,13824]{1,0:T(8,128)S(1)} %mul.3484, f32[16,13824]{1,0:T(8,128)S(1)} %reshape.616), kind=kOutput, calls=%fused_computation.9 | convolution fusion | flops 16146528 | bytes 2101632 | tf_op jit(solution)/shard_map/pq,cq->pc/dot_general | solution.py:159
  191.5 2.0 stack.173
  193.5 14.8 %all-to-all-done.1 = f32[32,16,128]{2,1,0:T(8,128)S(1)} async-done(((f32[32,16,128]{2,1,0:T(8,128)}), f32[32,16,128]{2,1,0:T(8,128)S(1)}, u32[]{:S(2)}, u32[]{:S(2)}) %all-to-all-start.1) | async-done | bytes 262176 | tf_op jit(solution)/shard_map/all_to_all | solution.py:163
  (163 shorter events, 43.2 us)
Async XLA Ops:
  0.6 159.3 %copy-start = (f32[9,16]{1,0:T(8,128)S(1)}, f32[9,16]{1,0:T(8,128)}, u32[]{:S(2)}) copy-start(f32[9,16]{1,0:T(8,128)} %param.11) | copy-start | bytes 1732
  1.7 9.1 %collective-permute-start.9 = (f32[1,128,128]{2,1,0:T(8,128)S(1)}, f32[1,128,128]{2,1,0:T(8,128)S(1)}, u32[]{:S(2)}, u32[]{:S(2)}) collective-permute-start(f32[1,128,128]{2,1,0:T(8,128)S(1)} %get-tuple-element.28), channel_id=1, source_target_pairs={{32,0},{64,32},{96,64},{128,96},{160,128},{192,160},{224,192},{256... | collective-permute-start | bytes 196616 | tf_op jit(solution)/shard_map/ppermute | solution.py:29
  3.8 7.0 %collective-permute-start.8 = (f32[1,128,128]{2,1,0:T(8,128)S(1)}, f32[1,128,128]{2,1,0:T(8,128)S(1)}, u32[]{:S(2)}, u32[]{:S(2)}) collective-permute-start(f32[1,128,128]{2,1,0:T(8,128)S(1)} %get-tuple-element.27), channel_id=1, source_target_pairs={{0,32},{32,64},{64,96},{96,128},{128,160},{160,192},{192,224},{224... | collective-permute-start | bytes 196616 | tf_op jit(solution)/shard_map/ppermute | solution.py:26
  7.6 20.7 %copy-start.2 = (f32[512,128]{1,0:T(8,128)S(1)}, f32[512,128]{1,0:T(8,128)}, u32[]{:S(2)}) copy-start(f32[512,128]{1,0:T(8,128)} %param.6) | copy-start | bytes 786436
  7.6 20.7 %copy-start.7 = (f32[512]{0:T(512)S(1)}, f32[512]{0:T(512)}, u32[]{:S(2)}) copy-start(f32[512]{0:T(512)} %param.9) | copy-start | bytes 6148
  11.1 7.6 %collective-permute-start.11 = (f32[1,128,128]{2,1,0:T(8,128)S(1)}, f32[1,128,128]{2,1,0:T(8,128)S(1)}, u32[]{:S(2)}, u32[]{:S(2)}) collective-permute-start(f32[1,128,128]{2,1,0:T(8,128)S(1)} %get-tuple-element.26), channel_id=1, source_target_pairs={{32,0},{64,32},{96,64},{128,96},{160,128},{192,160},{224,192},{256... | collective-permute-start | bytes 196616 | tf_op jit(solution)/shard_map/ppermute | solution.py:29
  14.4 5.6 %collective-permute-start.10 = (f32[1,128,128]{2,1,0:T(8,128)S(1)}, f32[1,128,128]{2,1,0:T(8,128)S(1)}, u32[]{:S(2)}, u32[]{:S(2)}) collective-permute-start(f32[1,128,128]{2,1,0:T(8,128)S(1)} %get-tuple-element.25), channel_id=1, source_target_pairs={{0,32},{32,64},{64,96},{96,128},{128,160},{160,192},{192,224},{224... | collective-permute-start | bytes 196616 | tf_op jit(solution)/shard_map/ppermute | solution.py:26
  20.3 7.7 %collective-permute-start.13 = (f32[1,128,128]{2,1,0:T(8,128)S(1)}, f32[1,128,128]{2,1,0:T(8,128)S(1)}, u32[]{:S(2)}, u32[]{:S(2)}) collective-permute-start(f32[1,128,128]{2,1,0:T(8,128)S(1)} %get-tuple-element.24), channel_id=1, source_target_pairs={{32,0},{64,32},{96,64},{128,96},{160,128},{192,160},{224,192},{256... | collective-permute-start | bytes 196616 | tf_op jit(solution)/shard_map/ppermute | solution.py:29
  22.2 6.1 %collective-permute-start.12 = (f32[1,128,128]{2,1,0:T(8,128)S(1)}, f32[1,128,128]{2,1,0:T(8,128)S(1)}, u32[]{:S(2)}, u32[]{:S(2)}) collective-permute-start(f32[1,128,128]{2,1,0:T(8,128)S(1)} %get-tuple-element.23), channel_id=1, source_target_pairs={{0,32},{32,64},{64,96},{96,128},{128,160},{160,192},{192,224},{224... | collective-permute-start | bytes 196616 | tf_op jit(solution)/shard_map/ppermute | solution.py:26
  28.7 17.1 %collective-permute-start.1 = (f32[1,128,128]{2,1,0:T(8,128)S(1)}, f32[1,128,128]{2,1,0:T(8,128)S(1)}, u32[]{:S(2)}, u32[]{:S(2)}) collective-permute-start(f32[1,128,128]{2,1,0:T(8,128)S(1)} %slice.173), channel_id=1, source_target_pairs={{0,32},{32,64},{64,96},{96,128},{128,160},{160,192},{192,224},{224... | collective-permute-start | bytes 196616 | tf_op jit(solution)/shard_map/ppermute | solution.py:36
  35.5 10.3 %collective-permute-start = (f32[1,128,128]{2,1,0:T(8,128)S(1)}, f32[1,128,128]{2,1,0:T(8,128)S(1)}, u32[]{:S(2)}, u32[]{:S(2)}) collective-permute-start(f32[1,128,128]{2,1,0:T(8,128)S(1)} %slice.172), channel_id=1, source_target_pairs={{0,480},{32,0},{64,32},{96,64},{128,96},{160,128},{192,160},{224,1... | collective-permute-start | bytes 196616 | tf_op jit(solution)/shard_map/ppermute | solution.py:36
  37.5 17.1 %collective-permute-start.15 = (f32[1,128,128]{2,1,0:T(8,128)S(1)}, f32[1,128,128]{2,1,0:T(8,128)S(1)}, u32[]{:S(2)}, u32[]{:S(2)}) collective-permute-start(f32[1,128,128]{2,1,0:T(8,128)S(1)} %get-tuple-element.22), channel_id=1, source_target_pairs={{32,0},{64,32},{96,64},{128,96},{160,128},{192,160},{224,192},{256... | collective-permute-start | bytes 196616 | tf_op jit(solution)/shard_map/ppermute | solution.py:29
  39.4 15.2 %collective-permute-start.14 = (f32[1,128,128]{2,1,0:T(8,128)S(1)}, f32[1,128,128]{2,1,0:T(8,128)S(1)}, u32[]{:S(2)}, u32[]{:S(2)}) collective-permute-start(f32[1,128,128]{2,1,0:T(8,128)S(1)} %get-tuple-element.21), channel_id=1, source_target_pairs={{0,32},{32,64},{64,96},{96,128},{128,160},{160,192},{192,224},{224... | collective-permute-start | bytes 196616 | tf_op jit(solution)/shard_map/ppermute | solution.py:26
  46.3 8.4 %collective-permute-start.3 = (f32[1,128,128]{2,1,0:T(8,128)S(1)}, f32[1,128,128]{2,1,0:T(8,128)S(1)}, u32[]{:S(2)}, u32[]{:S(2)}) collective-permute-start(f32[1,128,128]{2,1,0:T(8,128)S(1)} %slice.177), channel_id=1, source_target_pairs={{0,32},{32,64},{64,96},{96,128},{128,160},{160,192},{192,224},{224... | collective-permute-start | bytes 196616 | tf_op jit(solution)/shard_map/ppermute | solution.py:36
  52.0 3.8 %collective-permute-start.2 = (f32[1,128,128]{2,1,0:T(8,128)S(1)}, f32[1,128,128]{2,1,0:T(8,128)S(1)}, u32[]{:S(2)}, u32[]{:S(2)}) collective-permute-start(f32[1,128,128]{2,1,0:T(8,128)S(1)} %slice.176), channel_id=1, source_target_pairs={{0,480},{32,0},{64,32},{96,64},{128,96},{160,128},{192,160},{224,1... | collective-permute-start | bytes 196616 | tf_op jit(solution)/shard_map/ppermute | solution.py:36
  56.7 8.3 %collective-permute-start.5 = (f32[1,128,128]{2,1,0:T(8,128)S(1)}, f32[1,128,128]{2,1,0:T(8,128)S(1)}, u32[]{:S(2)}, u32[]{:S(2)}) collective-permute-start(f32[1,128,128]{2,1,0:T(8,128)S(1)} %slice.181), channel_id=1, source_target_pairs={{0,32},{32,64},{64,96},{96,128},{128,160},{160,192},{192,224},{224... | collective-permute-start | bytes 196616 | tf_op jit(solution)/shard_map/ppermute | solution.py:36
  63.0 3.8 %collective-permute-start.4 = (f32[1,128,128]{2,1,0:T(8,128)S(1)}, f32[1,128,128]{2,1,0:T(8,128)S(1)}, u32[]{:S(2)}, u32[]{:S(2)}) collective-permute-start(f32[1,128,128]{2,1,0:T(8,128)S(1)} %slice.180), channel_id=1, source_target_pairs={{0,480},{32,0},{64,32},{96,64},{128,96},{160,128},{192,160},{224,1... | collective-permute-start | bytes 196616 | tf_op jit(solution)/shard_map/ppermute | solution.py:36
  67.6 45.1 %collective-permute-start.7 = (f32[1,128,128]{2,1,0:T(8,128)S(1)}, f32[1,128,128]{2,1,0:T(8,128)S(1)}, u32[]{:S(2)}, u32[]{:S(2)}) collective-permute-start(f32[1,128,128]{2,1,0:T(8,128)S(1)} %slice.185), channel_id=1, source_target_pairs={{0,32},{32,64},{64,96},{96,128},{128,160},{160,192},{192,224},{224... | collective-permute-start | bytes 196616 | tf_op jit(solution)/shard_map/ppermute | solution.py:36
  73.4 39.3 %collective-permute-start.6 = (f32[1,128,128]{2,1,0:T(8,128)S(1)}, f32[1,128,128]{2,1,0:T(8,128)}, u32[]{:S(2)}, u32[]{:S(2)}) collective-permute-start(f32[1,128,128]{2,1,0:T(8,128)S(1)} %slice.184), channel_id=1, source_target_pairs={{0,480},{32,0},{64,32},{96,64},{128,96},{160,128},{192,160},{224,1... | collective-permute-start | bytes 196616 | tf_op jit(solution)/shard_map/ppermute | solution.py:36
  76.1 32.7 %all-to-all-start.3 = ((f32[32,16,1]{1,2,0:T(1,128)}), f32[32,16,1]{1,2,0:T(1,128)S(1)}, u32[]{:S(2)}, u32[]{:S(2)}) async-start(f32[32,16,1]{1,2,0:T(1,128)} %bitcast.60), calls=%async_computation.3 | async-start | bytes 32768 | tf_op jit(solution)/shard_map/all_to_all | solution.py:144
  94.1 44.1 %copy-start.4 = (f32[1,13824]{1,0:T(1,128)S(1)}, f32[1,13824]{1,0:T(1,128)}, u32[]{:S(2)}) copy-start(f32[1,13824]{1,0:T(1,128)} %get-tuple-element.33) | copy-start | bytes 165892
  94.1 44.1 %copy-start.5 = (f32[1,13824]{1,0:T(1,128)S(1)}, f32[1,13824]{1,0:T(1,128)}, u32[]{:S(2)}) copy-start(f32[1,13824]{1,0:T(1,128)} %get-tuple-element.9) | copy-start | bytes 165892
  108.8 21.7 %copy-start.6 = (f32[32,16,1]{1,2,0:T(1,128)}, f32[32,16,1]{1,2,0:T(1,128)S(1)}, u32[]{:S(2)}) copy-start(f32[32,16,1]{1,2,0:T(1,128)S(1)} %all-to-all-done.3) | copy-start | bytes 6148
  108.8 21.7 %all-to-all-start.2 = ((bf16[32,16,128]{2,1,0:T(8,128)(2,1)}), bf16[32,16,128]{2,1,0:T(8,128)(2,1)S(1)}, u32[]{:S(2)}, u32[]{:S(2)}) async-start(bf16[32,16,128]{2,1,0:T(8,128)(2,1)} %bitcast.52), calls=%async_computation.2 | async-start | bytes 262144 | tf_op jit(solution)/shard_map/all_to_all | solution.py:146
  112.7 26.8 %copy-start.9 = (f32[1,24]{1,0:T(1,128)S(1)}, f32[1,24]{1,0:T(1,128)}, u32[]{:S(2)}) copy-start(f32[1,24]{1,0:T(1,128)} %get-tuple-element.69) | copy-start | bytes 292
  112.7 26.8 %copy-start.10 = (f32[1,24]{1,0:T(1,128)S(1)}, f32[1,24]{1,0:T(1,128)}, u32[]{:S(2)}) copy-start(f32[1,24]{1,0:T(1,128)} %get-tuple-element.70) | copy-start | bytes 292
  112.7 26.8 %copy-start.11 = (f32[1,24]{1,0:T(1,128)S(1)}, f32[1,24]{1,0:T(1,128)}, u32[]{:S(2)}) copy-start(f32[1,24]{1,0:T(1,128)} %get-tuple-element.67) | copy-start | bytes 292
  112.7 26.8 %copy-start.12 = (f32[1,24]{1,0:T(1,128)S(1)}, f32[1,24]{1,0:T(1,128)}, u32[]{:S(2)}) copy-start(f32[1,24]{1,0:T(1,128)} %get-tuple-element.68) | copy-start | bytes 292
  112.7 26.8 %copy-start.13 = (f32[1,24]{1,0:T(1,128)S(1)}, f32[1,24]{1,0:T(1,128)}, u32[]{:S(2)}) copy-start(f32[1,24]{1,0:T(1,128)} %get-tuple-element.65) | copy-start | bytes 292
  112.7 26.8 %copy-start.14 = (f32[1,24]{1,0:T(1,128)S(1)}, f32[1,24]{1,0:T(1,128)}, u32[]{:S(2)}) copy-start(f32[1,24]{1,0:T(1,128)} %get-tuple-element.66) | copy-start | bytes 292
  130.5 26.1 %all-to-all-start = ((f32[32,16,128]{2,1,0:T(8,128)}), f32[32,16,128]{2,1,0:T(8,128)S(1)}, u32[]{:S(2)}, u32[]{:S(2)}) async-start(f32[32,16,128]{2,1,0:T(8,128)} %bitcast.13), calls=%async_computation | async-start | bytes 524288 | tf_op jit(solution)/shard_map/all_to_all | solution.py:143
  183.2 25.1 %all-to-all-start.1 = ((f32[32,16,128]{2,1,0:T(8,128)}), f32[32,16,128]{2,1,0:T(8,128)S(1)}, u32[]{:S(2)}, u32[]{:S(2)}) async-start(f32[32,16,128]{2,1,0:T(8,128)} %constant_dynamic-update-slice_fusion), calls=%async_computation.1 | async-start | bytes 524288 | tf_op jit(solution)/shard_map/all_to_all | solution.py:163
  (3 other events, 32.7 us)
